TPU v7x, 768 devices: a whole 4x8x12 slice. The times are simulated.
768 devices in a mesh: space: 96 (over z, y), members: 8 (over x, core).
Axes of the slice: x: 4, y: 8, z: 12, core: 2. Of those that a mesh axis runs over, the one named last changes fastest.
Arguments:
- alpha: bfloat16 [2, 80, 768, 128], P(None, 'members', 'space'), may hold values from -6 to 6
- kernel: bfloat16 [1152, 128, 128], P('space'), may hold values from -0.5 to 0.5
- src_index: int32 [1152], P('space'), may hold values from 4 to 19, as said below
- dst_index: int32 [1152], P('space'), may hold values from 0 to 7
- entry_count: int32 [96], P('space'), may hold values from 6 to 12, as said below
- interp_index: int32 [4, 1769472], P(None, 'space'), may hold values from 0 to 1023
- interp_weight: float32 [4, 1769472], P(None, 'space'), may hold values from 0.1 to 1
- perturbation: bfloat16 [2, 80, 1769472], P(None, 'members', 'space'), may hold values from -0.625 to 0.625
Outputs:
- increment: float32 [2, 1769472], P(None, ('space', 'members'))
Inputs may be any that keep to these rules, and one draw needn't show every extreme that they name: `src_index`: live entries read either the last 4 blocks of the previous tile, any block of the own tile, or the first 4 blocks of the next tile; padded entries read the own tile's first block. `entry_count`: some tile has all 12 entries live.
All inputs are finite; a program needn't handle non-finite values.
Results may differ from a plain program's by a relative error of at most 0.0029.
Values may be sent and summed in bfloat16 or wider, within the bound.
A program may use at most 128 MiB of HBM per device.

v0:
```python
import jax
import jax.numpy as jnp
from jax import lax
from jax.sharding import PartitionSpec as P


def shifted(value, axis, steps):
    count = lax.axis_size(axis)
    pairs = [(source, (source + steps) % count) for source in range(count)]
    return lax.ppermute(value, axis, pairs)


def per_device(
    alpha, kernel, src_index, dst_index, entry_count, interp_index, interp_weight, perturbation
):
    levels = alpha.shape[0]
    group = alpha.shape[1]
    blocks = alpha.shape[2]
    width = alpha.shape[3]
    entries = kernel.shape[0]
    received = []
    for offset, piece in ((1, alpha), (-1, alpha)):
        received.append(shifted(piece, "space", offset))
    window = jnp.concatenate([received[0], alpha, received[1]], axis=2)
    window_blocks = window.shape[2]
    picker = (src_index[:, None] == jnp.arange(window_blocks, dtype=jnp.int32)[None, :]).astype(
        jnp.bfloat16
    )
    pieces = jnp.einsum("lmsq,ps->lmpq", window, picker, preferred_element_type=jnp.float32).astype(
        jnp.bfloat16
    )
    product = jnp.einsum("lmpq,pqr->lmpr", pieces, kernel, preferred_element_type=jnp.float32)
    live = (jnp.arange(entries, dtype=jnp.int32) < entry_count[0]).astype(jnp.float32)
    onehot = (dst_index[:, None] == jnp.arange(blocks, dtype=jnp.int32)[None, :]).astype(
        jnp.float32
    ) * live[:, None]
    summed = jnp.einsum("lmpr,pj->lmjr", product, onehot, precision=lax.Precision.HIGHEST)
    conv_rows = summed.astype(jnp.bfloat16).reshape(levels, group, blocks * width)
    values = jnp.take(conv_rows, interp_index, axis=2)
    interpolated = jnp.sum(values.astype(jnp.float32) * interp_weight[None, None], axis=2)
    partial_sum = jnp.sum(perturbation.astype(jnp.float32) * interpolated, axis=1)
    return lax.psum_scatter(partial_sum, "members", scatter_dimension=1, tiled=True)


def solution(mesh):
    return jax.shard_map(
        per_device,
        mesh=mesh,
        in_specs=(
            P(None, "members", "space", None),
            P("space", None, None),
            P("space"),
            P("space"),
            P("space"),
            P(None, "space"),
            P(None, "space"),
            P(None, "members", "space"),
        ),
        out_specs=P(None, ("space", "members")),
        check_vma=False,
    )
```

profile of v0, /device:TPU:1, one launch (start us, length us, event | category | flops | bytes accessed | tf_op | source)
XLA Modules:
  0.0 673.4 jit_solution(13707786056882121713)
XLA Ops:
  6.5 0.0 copy-start
  6.5 0.0 copy-start.2
  6.5 0.0 reduce-scatter.4.cloned.1.call-start
  6.5 4.2 collective-permute-start
  10.7 15.9 %collective-permute-start.1 = (bf16[2,10,8,128]{3,2,1,0:T(8,128)(2,1)}, bf16[2,10,8,128]{3,2,1,0:T(8,128)(2,1)S(1)}, u32[]{:S(2)}, u32[]{:S(2)}) collective-permute-start(bf16[2,10,8,128]{3,2,1,0:T(8,128)(2,1)} %param.8), channel_id=1, source_target_pairs={{0,760},{8,0},{16,8},{24,16},{32,24},{40,32},{48,40},{56,48},{64,5... | collective-permute-start | bytes 122888 | tf_op jit(solution)/shard_map/ppermute | solution.py:10
  26.6 1.0 fusion.4
  27.7 1.1 compare_and_fusion
  29.6 0.0 collective-permute-done
  29.6 0.0 collective-permute-done.1
  29.6 1.0 fusion.1
  30.6 0.0 copy-done
  30.6 0.2 convolution_bitcast_fusion
  30.8 0.0 copy-done.2
  30.8 0.3 fusion.2
  31.1 0.3 copy.25
  31.4 474.9 %gather_fusion = bf16[73728,2,10]{2,1,0:T(2,128)(2,1)} fusion(bf16[2,10,1024]{1,0,2:T(2,128)(2,1)S(1)} %bitcast.36, s32[73728]{0:T(1024)S(1)} %broadcast_clamp_fusion), kind=kCustom, calls=%fused_computation | custom fusion | bytes 6193152 | tf_op jit(solution)/shard_map/jit(_take)/gather | solution.py:39
  506.3 86.2 %copy.22 = bf16[4,18432,2,10]{1,0,2,3:T(4,128)(2,1)S(1)} copy(bf16[4,18432,2,10]{3,2,1,0:T(2,128)(2,1)} %bitcast.34) | data formatting | bytes 5898240 | tf_op jit(solution)/shard_map/jit(_take)/gather | solution.py:39
  592.6 0.0 copy-start.1
  592.6 6.1 multiply_reduce_fusion
  598.7 0.0 copy-done.1
  598.7 0.8 fusion
  599.5 5.0 copy.23
  604.6 0.0 reduce-scatter.4.cloned.1.call-update
  604.6 59.7 %reduce-scatter.4.cloned.1.call-done = f32[2304,2]{1,0:T(8,128)} async-done(((f32[18432,2]{1,0:T(8,128)}), f32[2304,2]{1,0:T(8,128)}) %reduce-scatter.4.cloned.1.call-update) | async-done | bytes 18448
  664.3 2.2 copy.24
  (3 shorter events, 0.1 us)
Async XLA Ops:
  6.5 24.1 %copy-start = (bf16[12,128,128]{2,1,0:T(8,128)(2,1)S(1)}, bf16[12,128,128]{2,1,0:T(8,128)(2,1)}, u32[]{:S(2)}) copy-start(bf16[12,128,128]{2,1,0:T(8,128)(2,1)} %param.9) | copy-start | bytes 1179652
  6.5 24.3 %copy-start.2 = (s32[12]{0:T(128)S(1)}, s32[12]{0:T(128)}, u32[]{:S(2)}) copy-start(s32[12]{0:T(128)} %param.11) | copy-start | bytes 148
  6.5 657.8 %reduce-scatter.4.cloned.1.call-start = ((), (), s32[]{:S(2)}) async-start(), calls=%async_computation.1 | async-start | bytes 10616832
  6.5 23.0 %collective-permute-start = (bf16[2,10,8,128]{3,2,1,0:T(8,128)(2,1)}, bf16[2,10,8,128]{3,2,1,0:T(8,128)(2,1)S(1)}, u32[]{:S(2)}, u32[]{:S(2)}) collective-permute-start(bf16[2,10,8,128]{3,2,1,0:T(8,128)(2,1)} %param.8), channel_id=1, source_target_pairs={{0,8},{8,16},{16,24},{24,32},{32,40},{40,48},{48,56},{56,64},{64,7... | collective-permute-start | bytes 122888 | tf_op jit(solution)/shard_map/ppermute | solution.py:10
  10.7 18.9 %collective-permute-start.1 = (bf16[2,10,8,128]{3,2,1,0:T(8,128)(2,1)}, bf16[2,10,8,128]{3,2,1,0:T(8,128)(2,1)S(1)}, u32[]{:S(2)}, u32[]{:S(2)}) collective-permute-start(bf16[2,10,8,128]{3,2,1,0:T(8,128)(2,1)} %param.8), channel_id=1, source_target_pairs={{0,760},{8,0},{16,8},{24,16},{32,24},{40,32},{48,40},{56,48},{64,5... | collective-permute-start | bytes 122888 | tf_op jit(solution)/shard_map/ppermute | solution.py:10
  592.6 6.1 copy-start.1
Sparse Core Ops, SparseCore 0:
  604.7 59.5 reduce-scatter.3
where the time goes:
time: 676 us; the launch traced here: 673 us
  local copies, waits for them, and re-layouts  569 us (84%)
  waiting for transfers between devices  59.8 us (9%)
  starting transfers between devices  20.1 us (3%)
  between operations  14.2 us (2%)
  other arithmetic  9.15 us (1%)
    gather x2, local copies, waits for them, and re-layouts, per_device(): values = jnp.take(conv_rows, interp_index, axis=2)  561 us
    unnamed x2, waiting for transfers between devices  59.8 us
    ppermute x2, starting transfers between devices, shifted(): return lax.ppermute(value, axis, pairs)  20.1 us
  transfers between devices with their start and end apart: 3, of which 1 were waited for; matrix products, arithmetic and copies ran while one was open for 0% of the time, Pallas kernels for 0%

commit v1 on v0

v1 whole, which is shorter than its diff:
```python
import jax
import jax.numpy as jnp
from jax import lax
from jax.experimental import pallas as pl
from jax.experimental.pallas import tpu as pltpu
from jax.sharding import PartitionSpec as P

MESH = pl.DeviceIdType.MESH
LANES = 128


def halo_kernel(alpha_ref, prev_ref, next_ref, send_sem, recv_sem):
    count = lax.axis_size("space")
    me = lax.axis_index("space")
    right, left = lax.rem(me + 1, count), lax.rem(me + count - 1, count)
    barrier = pltpu.get_barrier_semaphore()
    for neighbour in (left, right):
        pl.semaphore_signal(barrier, inc=1, device_id={"space": neighbour}, device_id_type=MESH)
    pl.semaphore_wait(barrier, 2)
    copies = []
    for way, (neighbour, landing) in enumerate(((right, prev_ref), (left, next_ref))):
        copy = pltpu.make_async_remote_copy(
            src_ref=alpha_ref,
            dst_ref=landing,
            send_sem=send_sem.at[way],
            recv_sem=recv_sem.at[way],
            device_id={"space": neighbour},
            device_id_type=MESH,
        )
        copy.start()
        copies.append(copy)
    for copy in copies:
        copy.wait()


def exchange_halo(alpha):
    vmem = pl.BlockSpec(memory_space=pltpu.VMEM)
    shape = jax.ShapeDtypeStruct(alpha.shape, alpha.dtype)
    return pl.pallas_call(
        halo_kernel,
        out_shape=(shape, shape),
        in_specs=[vmem],
        out_specs=(vmem, vmem),
        scratch_shapes=[pltpu.SemaphoreType.DMA((2,)), pltpu.SemaphoreType.DMA((2,))],
        compiler_params=pltpu.CompilerParams(
            collective_id=0, has_side_effects=True, vmem_limit_bytes=8 * 1024 * 1024
        ),
    )(alpha)


def convolve(src_ref, dst_ref, count_ref, sides, kernel_ref, window, sums, table):
    levels, members, blocks, _ = sides[0].shape
    lm = levels * members
    rows = lm * blocks
    for side, ref in enumerate(sides):
        for l in range(levels):
            for m in range(members):
                at = side * rows + (m * levels + l) * blocks
                window[at:at + blocks, :] = ref[l, m].astype(jnp.float32)
    sums[...] = jnp.zeros_like(sums)
    for e in range(kernel_ref.shape[0]):
        s = src_ref[e]
        start = (s // blocks) * rows + s % blocks
        piece = window[pl.ds(start, lm, stride=blocks), :].astype(jnp.bfloat16)
        product = jnp.dot(piece, kernel_ref[e], preferred_element_type=jnp.float32)
        live = jnp.where(e < count_ref[0], 1.0, 0.0).astype(jnp.float32)
        d = dst_ref[e]
        sums[d] = sums[d] + product * live
    half = blocks // 2
    for j in range(blocks):
        table[j // half, pl.ds(j % half, lm, stride=half), :] = sums[j]


def interpolate(table, index_ref, weight_ref, pert_ref, out_ref):
    members, levels, _ = pert_ref.shape
    owners, _, span = out_ref.shape
    half = table.shape[1] // (members * levels)
    depth = 2 * LANES
    left = jnp.concatenate([table[0], table[1]], axis=1).astype(jnp.bfloat16)

    def body(g, carry):
        cols = pl.ds(pl.multiple_of(g * span, LANES), span)
        sub = lax.broadcasted_iota(jnp.int32, (levels * half, span), 0) % half
        points = lax.broadcasted_iota(jnp.int16, (depth, span), 0)
        total = None
        for k in range(index_ref.shape[0]):
            index = index_ref[pl.ds(k, 1), cols]
            weight = jnp.broadcast_to(weight_ref[pl.ds(k, 1), cols], (levels * half, span))
            block = index >> 7
            place = (block // half) * LANES + (index & (LANES - 1))
            row = jnp.broadcast_to(block % half, (levels * half, span))
            masked = jnp.where(row == sub, weight, 0.0)
            place = jnp.broadcast_to(place, (16, span)).astype(jnp.int16)[0:1]
            hot = jnp.where(
                points == jnp.broadcast_to(place, (depth, span)), jnp.bfloat16(1), jnp.bfloat16(0)
            )
            values = jnp.dot(left, hot, preferred_element_type=jnp.float32)
            values = values.reshape(members, levels * half, span) * masked[None]
            total = values if k == 0 else total + values
        summed = None
        for m in range(members):
            p = pert_ref[m, :, cols].astype(jnp.float32)
            wide = jnp.concatenate(
                [jnp.broadcast_to(p[l:l + 1], (half, span)) for l in range(levels)], axis=0
            )
            summed = total[m] * wide if m == 0 else summed + total[m] * wide
        out_ref[g] = jnp.concatenate(
            [jnp.sum(summed[l * half:(l + 1) * half], axis=0, keepdims=True) for l in range(levels)], axis=0
        )
        return carry

    lax.fori_loop(0, owners, body, 0)


def local_kernel(
    src_ref, dst_ref, count_ref, prev_ref, alpha_ref, next_ref, kernel_ref, index_ref, weight_ref, pert_ref,
    out_ref, window, sums, table, kernel_vmem, index_vmem, weight_vmem, pert_vmem, load_sem,
):
    loads = []
    pairs = ((kernel_ref, kernel_vmem), (index_ref, index_vmem), (weight_ref, weight_vmem), (pert_ref, pert_vmem))
    for number, (source, target) in enumerate(pairs):
        load = pltpu.make_async_copy(source, target, load_sem.at[number])
        load.start()
        loads.append(load)
    loads[0].wait()
    convolve(src_ref, dst_ref, count_ref, (prev_ref, alpha_ref, next_ref), kernel_vmem, window, sums, table)
    for load in loads[1:]:
        load.wait()
    interpolate(table, index_vmem, weight_vmem, pert_vmem, out_ref)


def local_increment(owners, prev, alpha, following, kernel, src, dst, count, index, weight, pert):
    levels, members, blocks, width = alpha.shape
    lm = levels * members
    smem = pl.BlockSpec(memory_space=pltpu.SMEM)
    vmem = pl.BlockSpec(memory_space=pltpu.VMEM)
    return pl.pallas_call(
        local_kernel,
        out_shape=jax.ShapeDtypeStruct((owners, levels, index.shape[1] // owners), jnp.float32),
        in_specs=[smem] * 3 + [vmem] * 3 + [pl.BlockSpec(memory_space=pl.ANY)] * 4,
        out_specs=vmem,
        scratch_shapes=[
            pltpu.VMEM((3 * lm * blocks, width), jnp.float32),
            pltpu.VMEM((blocks, lm, width), jnp.float32),
            pltpu.VMEM((2, lm * blocks // 2, width), jnp.float32),
            pltpu.VMEM(kernel.shape, kernel.dtype),
            pltpu.VMEM(index.shape, index.dtype),
            pltpu.VMEM(weight.shape, weight.dtype),
            pltpu.VMEM((members, levels, index.shape[1]), pert.dtype),
            pltpu.SemaphoreType.DMA((4,)),
        ],
        compiler_params=pltpu.CompilerParams(vmem_limit_bytes=60 * 1024 * 1024),
    )(src, dst, count, prev, alpha, following, kernel, index, weight, jnp.transpose(pert, (1, 0, 2)))


def share_kernel(owners, partial_ref, out_ref, slots, send_sem, recv_sem):
    me = lax.axis_index("members")
    barrier = pltpu.get_barrier_semaphore()
    for step in range(1, owners):
        peer = lax.rem(me + step, owners)
        pl.semaphore_signal(barrier, inc=1, device_id={"members": peer}, device_id_type=MESH)
    pl.semaphore_wait(barrier, owners - 1)
    copies = []
    for step in range(1, owners):
        peer = lax.rem(me + step, owners)
        copy = pltpu.make_async_remote_copy(
            src_ref=partial_ref.at[peer],
            dst_ref=slots.at[step - 1],
            send_sem=send_sem.at[step - 1],
            recv_sem=recv_sem.at[step - 1],
            device_id={"members": peer},
            device_id_type=MESH,
        )
        copy.start()
        copies.append(copy)
    total = partial_ref[me]
    for step, copy in enumerate(copies):
        copy.wait_recv()
        total = total + slots[step]
    out_ref[...] = total
    for copy in copies:
        copy.wait_send()


def share_increment(partial):
    owners, levels, span = partial.shape
    vmem = pl.BlockSpec(memory_space=pltpu.VMEM)
    return pl.pallas_call(
        lambda *refs: share_kernel(owners, *refs),
        out_shape=jax.ShapeDtypeStruct((levels, span), jnp.float32),
        in_specs=[vmem],
        out_specs=vmem,
        scratch_shapes=[
            pltpu.VMEM((owners - 1, levels, span), jnp.float32),
            pltpu.SemaphoreType.DMA((owners - 1,)),
            pltpu.SemaphoreType.DMA((owners - 1,)),
        ],
        compiler_params=pltpu.CompilerParams(
            collective_id=1, has_side_effects=True, vmem_limit_bytes=8 * 1024 * 1024
        ),
    )(partial)


def per_device(
    alpha, kernel, src_index, dst_index, entry_count, interp_index, interp_weight, perturbation
):
    owners = lax.axis_size("members")
    prev, following = exchange_halo(alpha)
    partial = local_increment(
        owners, prev, alpha, following, kernel, src_index, dst_index, entry_count,
        interp_index, interp_weight, perturbation,
    )
    return share_increment(partial)


def solution(mesh):
    return jax.shard_map(
        per_device,
        mesh=mesh,
        in_specs=(
            P(None, "members", "space", None),
            P("space", None, None),
            P("space"),
            P("space"),
            P("space"),
            P(None, "space"),
            P(None, "space"),
            P(None, "members", "space"),
        ),
        out_specs=P(None, ("space", "members")),
        check_vma=False,
    )
```

time: 676 us -> 44.5 us (0.07)
  local copies, waits for them, and re-layouts: 569 us -> 3.5 us
  waiting for transfers between devices: 59.8 us -> 0 us
  Pallas kernels: 0 us -> 39.9 us
  starting transfers between devices: 20.1 us -> 0 us
  between operations: 14.2 us -> 0.7 us
  other arithmetic: 9.15 us -> 0 us
    gather x2 -> x0, local copies, waits for them, and re-layouts: 561 us -> none  [per_device(): values = jnp.take(conv_rows, interp_index, axis=2)]
    unnamed x2 -> x0, waiting for transfers between devices: 59.8 us -> none
    pallas_call x0 -> x3, Pallas kernels: none -> 39.9 us  [the longest x1 19.4 us: exchange_halo(): pl.pallas_call(halo_kernel, out_shape=(shape, shape), in_specs=[vmem], ou...]
    ppermute x2 -> x0, starting transfers between devices: 20.1 us -> none  [shifted(): return lax.ppermute(value, axis, pairs)]
    reduce_sum x2 -> x0, other arithmetic: 6.92 us -> none  [the longest x1 6.07 us: per_device(): jnp.sum(values.astype(jnp.float32) * interp_weight[None, None], axis=2)]
  transfers between devices with their start and end apart: 3 -> 0, of which waited for: 1 -> 0; matrix products, arithmetic and copies ran while one was open for 0% -> 0% of each run, Pallas kernels for 0% -> 0%
where the time goes in v1:
time: 44.5 us; the launch traced here: 44.1 us
  Pallas kernels  39.9 us (90%)
  local copies, waits for them, and re-layouts  3.5 us (8%)
  between operations  0.7 us (2%)
    pallas_call x1, Pallas kernels, exchange_halo(): pl.pallas_call(halo_kernel, out_shape=(shape, shape), in_specs=[vmem], ou...  19.4 us
    pallas_call x1, Pallas kernels, local_increment(): pl.pallas_call(local_kernel, out_shape=jax.ShapeDtypeStruct((owners, leve...  11.6 us
    pallas_call x1, Pallas kernels, share_increment(): pl.pallas_call(lambda *refs: share_kernel(owners, *refs), out_shape=jax.S...  8.93 us
    unnamed x9, local copies, waits for them, and re-layouts  3.5 us

profile of v1, /device:TPU:1, one launch (start us, length us, event | category | flops | bytes accessed | tf_op | source)
XLA Modules:
  0.0 44.1 jit_solution(17895957044310680491)
XLA Ops:
  0.7 0.0 copy-start.1
  0.7 0.8 %copy-done.1 = bf16[2,10,8,128]{3,2,1,0:T(8,128)(2,1)S(1)} copy-done((bf16[2,10,8,128]{3,2,1,0:T(8,128)(2,1)S(1)}, bf16[2,10,8,128]{3,2,1,0:T(8,128)(2,1)}, u32[]{:S(2)}) %copy-start.1) | copy-done | bytes 40984
  1.4 19.4 %shard_map.82 = (bf16[2,10,8,128]{3,2,1,0:T(8,128)(2,1)S(1)}, bf16[2,10,8,128]{3,2,1,0:T(8,128)(2,1)S(1)}) custom-call(bf16[2,10,8,128]{3,2,1,0:T(8,128)(2,1)S(1)} %copy-done.1), custom_call_target="tpu_custom_call" | custom-call | tf_op jit(solution)/shard_map/pallas_call | solution.py:39
  20.8 0.0 copy-start.2
  20.8 0.6 %copy-done.2 = bf16[2,10,8,128]{3,2,1,0:T(8,128)(2,1)} copy-done((bf16[2,10,8,128]{3,2,1,0:T(8,128)(2,1)}, bf16[2,10,8,128]{3,2,1,0:T(8,128)(2,1)S(1)}, u32[]{:S(2)}) %copy-start.2) | copy-done | bytes 40984
  21.4 0.0 copy-start.3
  21.4 0.6 %copy-done.3 = bf16[2,10,8,128]{3,2,1,0:T(8,128)(2,1)} copy-done((bf16[2,10,8,128]{3,2,1,0:T(8,128)(2,1)}, bf16[2,10,8,128]{3,2,1,0:T(8,128)(2,1)S(1)}, u32[]{:S(2)}) %copy-start.3) | copy-done | bytes 40984
  22.0 11.6 %shard_map.83.refs_0_ = f32[8,2,2304]{2,1,0:T(2,128)} custom-call(s32[12]{0:T(128)} %src_ref.1, s32[12]{0:T(128)} %dst_ref.1, s32[1]{0:T(128)S(6)} %copy.10.count_ref, bf16[2,10,8,128]{3,2,1,0:T(8,128)(2,1)} %copy-done.2, bf16[2,10,8,128]{3,2,1,0:T(8,128)(2,1)} %alpha_ref.3, bf16[2,10,8,128]{3,2,1,0:T(8,128)(2,1)} %copy-done.3, ...), custom_call_target="tpu_custom_call" | custom-call | tf_op jit(solution)/shard_map/pallas_call | solution.py:137
  33.7 0.0 copy-start
  33.7 0.9 %copy-done = f32[8,2,2304]{2,1,0:T(2,128)S(1)} copy-done((f32[8,2,2304]{2,1,0:T(2,128)S(1)}, f32[8,2,2304]{2,1,0:T(2,128)}, u32[]{:S(2)}) %copy-start) | copy-done | bytes 147480
  34.6 8.9 %shard_map.84 = f32[2,2304]{1,0:T(2,128)S(1)} custom-call(f32[8,2,2304]{2,1,0:T(2,128)S(1)} %copy-done), custom_call_target="tpu_custom_call" | custom-call | tf_op jit(solution)/shard_map/pallas_call | solution.py:188
  43.5 0.6 %copy.11 = f32[2,2304]{1,0:T(2,128)} copy(f32[2,2304]{1,0:T(2,128)S(1)} %shard_map.84) | data formatting | bytes 36864
Async XLA Ops:
  0.7 0.8 %copy-start.1 = (bf16[2,10,8,128]{3,2,1,0:T(8,128)(2,1)S(1)}, bf16[2,10,8,128]{3,2,1,0:T(8,128)(2,1)}, u32[]{:S(2)}) copy-start(bf16[2,10,8,128]{3,2,1,0:T(8,128)(2,1)} %alpha_ref.3) | copy-start | bytes 122884
  20.8 0.6 %copy-start.2 = (bf16[2,10,8,128]{3,2,1,0:T(8,128)(2,1)}, bf16[2,10,8,128]{3,2,1,0:T(8,128)(2,1)S(1)}, u32[]{:S(2)}) copy-start(bf16[2,10,8,128]{3,2,1,0:T(8,128)(2,1)S(1)} %get-tuple-element.7.prev_ref) | copy-start | bytes 122884
  21.4 0.6 %copy-start.3 = (bf16[2,10,8,128]{3,2,1,0:T(8,128)(2,1)}, bf16[2,10,8,128]{3,2,1,0:T(8,128)(2,1)S(1)}, u32[]{:S(2)}) copy-start(bf16[2,10,8,128]{3,2,1,0:T(8,128)(2,1)S(1)} %get-tuple-element.8.next_ref) | copy-start | bytes 122884
  33.7 0.9 %copy-start = (f32[8,2,2304]{2,1,0:T(2,128)S(1)}, f32[8,2,2304]{2,1,0:T(2,128)}, u32[]{:S(2)}) copy-start(f32[8,2,2304]{2,1,0:T(2,128)} %shard_map.83.refs_0_) | copy-start | bytes 442372

commit v2 on v0

v2 whole, which is shorter than its diff:
```python
import jax
import jax.numpy as jnp
from jax import lax
from jax.experimental import pallas as pl
from jax.experimental.pallas import tpu as pltpu
from jax.sharding import PartitionSpec as P

MESH = pl.DeviceIdType.MESH
LANES = 128


def stage(ref, side, rows, window):
    levels, members, blocks, _ = ref.shape
    for l in range(levels):
        for m in range(members):
            at = (m * levels + l) * blocks
            rows[side, at:at + blocks, :] = ref[l, m].astype(jnp.float32)
    for j in range(blocks):
        window[side * blocks + j] = rows[side, pl.ds(j, levels * members, stride=blocks), :]


def convolve(src_ref, dst_ref, count_ref, blocks, kernel_ref, window, table):
    lm = window.shape[1]
    sums = [jnp.zeros((lm, LANES), jnp.float32) for _ in range(blocks)]
    for e in range(kernel_ref.shape[0]):
        piece = window[src_ref[e]].astype(jnp.bfloat16)
        product = jnp.dot(piece, kernel_ref[e], preferred_element_type=jnp.float32)
        live = jnp.where(e < count_ref[0], 1.0, 0.0).astype(jnp.float32)
        for j in range(blocks):
            factor = jnp.where(dst_ref[e] == j, live, 0.0)
            sums[j] = sums[j] + product * factor
    half = blocks // 2
    for j in range(blocks):
        table[j // half, pl.ds(j % half, lm, stride=half), :] = sums[j]


def interpolate(left, cols, index_ref, weight_ref, pert_ref):
    members, levels, _ = pert_ref.shape
    span = cols.size
    half = left.shape[0] // (members * levels)
    depth = 2 * LANES
    sub = lax.broadcasted_iota(jnp.int32, (levels * half, span), 0) % half
    points = lax.broadcasted_iota(jnp.int16, (depth, span), 0)
    total = None
    for k in range(index_ref.shape[0]):
        index = index_ref[pl.ds(k, 1), cols]
        weight = jnp.broadcast_to(weight_ref[pl.ds(k, 1), cols], (levels * half, span))
        block = index >> 7
        place = (block // half) * LANES + (index & (LANES - 1))
        row = jnp.broadcast_to(block % half, (levels * half, span))
        masked = jnp.where(row == sub, weight, 0.0)
        place = jnp.broadcast_to(place, (16, span)).astype(jnp.int16)[0:1]
        hot = jnp.where(
            points == jnp.broadcast_to(place, (depth, span)), jnp.bfloat16(1), jnp.bfloat16(0)
        )
        values = jnp.dot(left, hot, preferred_element_type=jnp.float32)
        values = values.reshape(members, levels * half, span) * masked[None]
        total = values if k == 0 else total + values
    summed = None
    for m in range(members):
        p = pert_ref[m, :, cols].astype(jnp.float32)
        wide = jnp.concatenate(
            [jnp.broadcast_to(p[l:l + 1], (half, span)) for l in range(levels)], axis=0
        )
        summed = total[m] * wide if m == 0 else summed + total[m] * wide
    return jnp.concatenate(
        [jnp.sum(summed[l * half:(l + 1) * half], axis=0, keepdims=True) for l in range(levels)], axis=0
    )


def whole_kernel(
    alpha_hbm, kernel_hbm, src_hbm, dst_hbm, count_hbm, index_hbm, weight_hbm, pert_hbm, out_ref,
    prev_ref, alpha_ref, next_ref, kernel_ref, src_ref, dst_ref, count_ref, index_ref, weight_ref, pert_ref,
    rows, window, table, partial, slots,
    load_sem, halo_send, halo_recv, share_send, share_recv,
):
    tiles, owners = lax.axis_size("space"), lax.axis_size("members")
    tile, me = lax.axis_index("space"), lax.axis_index("members")
    right, left = lax.rem(tile + 1, tiles), lax.rem(tile + tiles - 1, tiles)
    span = out_ref.shape[1]
    blocks = alpha_ref.shape[2]

    barrier = pltpu.get_barrier_semaphore()
    for neighbour in (left, right):
        pl.semaphore_signal(barrier, inc=1, device_id={"space": neighbour}, device_id_type=MESH)
    for step in range(1, owners):
        peer = lax.rem(me + step, owners)
        pl.semaphore_signal(barrier, inc=1, device_id={"members": peer}, device_id_type=MESH)

    loads = []
    for number, (source, target) in enumerate((
        (alpha_hbm, alpha_ref), (kernel_hbm, kernel_ref), (src_hbm, src_ref), (dst_hbm, dst_ref),
        (count_hbm, count_ref), (index_hbm, index_ref), (weight_hbm, weight_ref), (pert_hbm, pert_ref),
    )):
        load = pltpu.make_async_copy(source, target, load_sem.at[number])
        load.start()
        loads.append(load)

    pl.semaphore_wait(barrier, owners + 1)
    halos = []
    for way, (neighbour, landing) in enumerate(((right, prev_ref), (left, next_ref))):
        copy = pltpu.make_async_remote_copy(
            src_ref=alpha_hbm,
            dst_ref=landing,
            send_sem=halo_send.at[way],
            recv_sem=halo_recv.at[way],
            device_id={"space": neighbour},
            device_id_type=MESH,
        )
        copy.start()
        halos.append(copy)
    loads[0].wait()
    stage(alpha_ref, 1, rows, window)
    for load in loads[1:]:
        load.wait()
    halos[0].wait_recv()
    stage(prev_ref, 0, rows, window)
    halos[1].wait_recv()
    stage(next_ref, 2, rows, window)
    convolve(src_ref, dst_ref, count_ref, blocks, kernel_ref, window, table)

    def share(step):
        return pltpu.make_async_remote_copy(
            src_ref=partial.at[step - 1],
            dst_ref=slots.at[step - 1],
            send_sem=share_send.at[step - 1],
            recv_sem=share_recv.at[step - 1],
            device_id={"members": lax.rem(me + step, owners)},
            device_id_type=MESH,
        )

    def columns(owner):
        return pl.ds(pl.multiple_of(owner * span, LANES), span)

    matrix = jnp.concatenate([table[0], table[1]], axis=1).astype(jnp.bfloat16)

    def body(step, carry):
        cols = columns(lax.rem(me + step, owners))
        partial[step - 1] = interpolate(matrix, cols, index_ref, weight_ref, pert_ref)

        @pl.when(step < owners)
        def _():
            share(step).start()

        return carry

    lax.fori_loop(1, owners + 1, body, 0)
    total = partial[owners - 1]
    for step in range(1, owners):
        share(step).wait_recv()
        total = total + slots[step - 1]
    out_ref[...] = total
    for step in range(1, owners):
        share(step).wait_send()
    for copy in halos:
        copy.wait_send()


def per_device(
    alpha, kernel, src_index, dst_index, entry_count, interp_index, interp_weight, perturbation
):
    owners = lax.axis_size("members")
    levels, members, blocks, width = alpha.shape
    lm = levels * members
    span = interp_index.shape[1] // owners
    operands = (
        alpha, kernel, src_index, dst_index, entry_count, interp_index, interp_weight,
        jnp.transpose(perturbation, (1, 0, 2)),
    )
    return pl.pallas_call(
        whole_kernel,
        out_shape=jax.ShapeDtypeStruct((levels, span), jnp.float32),
        in_specs=[pl.BlockSpec(memory_space=pl.ANY)] * len(operands),
        out_specs=pl.BlockSpec(memory_space=pltpu.VMEM),
        scratch_shapes=[
            pltpu.VMEM(alpha.shape, alpha.dtype),
            pltpu.VMEM(alpha.shape, alpha.dtype),
            pltpu.VMEM(alpha.shape, alpha.dtype),
            pltpu.VMEM(kernel.shape, kernel.dtype),
            pltpu.SMEM(src_index.shape, src_index.dtype),
            pltpu.SMEM(dst_index.shape, dst_index.dtype),
            pltpu.SMEM(entry_count.shape, entry_count.dtype),
            pltpu.VMEM(interp_index.shape, interp_index.dtype),
            pltpu.VMEM(interp_weight.shape, interp_weight.dtype),
            pltpu.VMEM(operands[-1].shape, perturbation.dtype),
            pltpu.VMEM((3, lm * blocks, width), jnp.float32),
            pltpu.VMEM((3 * blocks, lm, width), jnp.float32),
            pltpu.VMEM((2, lm * blocks // 2, width), jnp.float32),
            pltpu.VMEM((owners, levels, span), jnp.float32),
            pltpu.VMEM((owners - 1, levels, span), jnp.float32),
            pltpu.SemaphoreType.DMA((len(operands),)),
            pltpu.SemaphoreType.DMA((2,)),
            pltpu.SemaphoreType.DMA((2,)),
            pltpu.SemaphoreType.DMA((owners - 1,)),
            pltpu.SemaphoreType.DMA((owners - 1,)),
        ],
        compiler_params=pltpu.CompilerParams(
            collective_id=0, has_side_effects=True, vmem_limit_bytes=60 * 1024 * 1024
        ),
    )(*operands)


def solution(mesh):
    return jax.shard_map(
        per_device,
        mesh=mesh,
        in_specs=(
            P(None, "members", "space", None),
            P("space", None, None),
            P("space"),
            P("space"),
            P("space"),
            P(None, "space"),
            P(None, "space"),
            P(None, "members", "space"),
        ),
        out_specs=P(None, ("space", "members")),
        check_vma=False,
    )
```

time: 676 us -> 35.6 us (0.05)
  local copies, waits for them, and re-layouts: 569 us -> 1.33 us
  waiting for transfers between devices: 59.8 us -> 0 us
  Pallas kernels: 0 us -> 33.4 us
  starting transfers between devices: 20.1 us -> 0 us
  between operations: 14.2 us -> 0.66 us
  other arithmetic: 9.15 us -> 0 us
    gather x2 -> x0, local copies, waits for them, and re-layouts: 561 us -> none  [per_device(): values = jnp.take(conv_rows, interp_index, axis=2)]
    unnamed x2 -> x0, waiting for transfers between devices: 59.8 us -> none
    pallas_call x0 -> x1, Pallas kernels: none -> 33.4 us  [per_device(): pl.pallas_call(whole_kernel, out_shape=jax.ShapeDtypeStruct((levels, span...]
    ppermute x2 -> x0, starting transfers between devices: 20.1 us -> none  [shifted(): return lax.ppermute(value, axis, pairs)]
    reduce_sum x2 -> x0, other arithmetic: 6.92 us -> none  [the longest x1 6.07 us: per_device(): jnp.sum(values.astype(jnp.float32) * interp_weight[None, None], axis=2)]
  transfers between devices with their start and end apart: 3 -> 0, of which waited for: 1 -> 0; matrix products, arithmetic and copies ran while one was open for 0% -> 0% of each run, Pallas kernels for 0% -> 0%
where the time goes in v2:
time: 35.6 us; the launch traced here: 35.4 us
  Pallas kernels  33.4 us (94%)
  local copies, waits for them, and re-layouts  1.33 us (4%)
  between operations  0.66 us (2%)
    pallas_call x1, Pallas kernels, per_device(): pl.pallas_call(whole_kernel, out_shape=jax.ShapeDtypeStruct((levels, span...  33.4 us
    unnamed x1, local copies, waits for them, and re-layouts  1.33 us

profile of v2, /device:TPU:1, one launch (start us, length us, event | category | flops | bytes accessed | tf_op | source)
XLA Modules:
  0.0 35.4 jit_solution(18136719894991176750)
XLA Ops:
  0.7 33.4 %shard_map.82 = f32[2,2304]{1,0:T(2,128)} custom-call(bf16[2,10,8,128]{3,2,1,0:T(8,128)(2,1)} %alpha_hbm.1, bf16[12,128,128]{2,1,0:T(8,128)(2,1)} %kernel_hbm.1, s32[12]{0:T(128)} %src_hbm.1, s32[12]{0:T(128)} %dst_hbm.1, s32[1]{0:T(128)S(6)} %copy.10.count_hbm, s32[4,18432]{1,0:T(4,128)} %index_hbm.1, f32[4,18432]{1,0:T(4,128)} %weight_hbm.1, ...), custom_call_target="tpu_custom_call" | custom-call | tf_op jit(solution)/shard_map/pallas_call | solution.py:170
  34.1 1.3 %copy.11 = f32[2,2304]{1,0:T(2,128)} copy(f32[2,2304]{1,0:T(2,128)} %shard_map.82) | data formatting | bytes 36864

commit v3 on v2

--- a/solution.py
+++ b/solution.py
@@ -7,14 +7,12 @@
 
 MESH = pl.DeviceIdType.MESH
 LANES = 128
+PIECE = 256
 
 
 def stage(ref, side, rows, window):
     levels, members, blocks, _ = ref.shape
-    for l in range(levels):
-        for m in range(members):
-            at = (m * levels + l) * blocks
-            rows[side, at:at + blocks, :] = ref[l, m].astype(jnp.float32)
+    rows[side] = ref[...].astype(jnp.float32).reshape(levels * members * blocks, LANES)
     for j in range(blocks):
         window[side * blocks + j] = rows[side, pl.ds(j, levels * members, stride=blocks), :]
 
@@ -29,43 +27,35 @@
         for j in range(blocks):
             factor = jnp.where(dst_ref[e] == j, live, 0.0)
             sums[j] = sums[j] + product * factor
-    half = blocks // 2
     for j in range(blocks):
-        table[j // half, pl.ds(j % half, lm, stride=half), :] = sums[j]
-
-
-def interpolate(left, cols, index_ref, weight_ref, pert_ref):
+        table[pl.ds(j, lm, stride=blocks), :] = sums[j]
+
+
+def interpolate(matrix, blocks, cols, index_ref, weight_ref, pert_ref):
     members, levels, _ = pert_ref.shape
     span = cols.size
-    half = left.shape[0] // (members * levels)
-    depth = 2 * LANES
-    sub = lax.broadcasted_iota(jnp.int32, (levels * half, span), 0) % half
-    points = lax.broadcasted_iota(jnp.int16, (depth, span), 0)
+    wide = (blocks, span)
+    sub = lax.broadcasted_iota(jnp.int32, wide, 0)
+    points = lax.broadcasted_iota(jnp.int16, (LANES, span), 0)
     total = None
     for k in range(index_ref.shape[0]):
         index = index_ref[pl.ds(k, 1), cols]
-        weight = jnp.broadcast_to(weight_ref[pl.ds(k, 1), cols], (levels * half, span))
-        block = index >> 7
-        place = (block // half) * LANES + (index & (LANES - 1))
-        row = jnp.broadcast_to(block % half, (levels * half, span))
-        masked = jnp.where(row == sub, weight, 0.0)
-        place = jnp.broadcast_to(place, (16, span)).astype(jnp.int16)[0:1]
+        weight = jnp.broadcast_to(weight_ref[pl.ds(k, 1), cols], wide)
+        masked = jnp.where(jnp.broadcast_to(index >> 7, wide) == sub, weight, 0.0)
+        place = jnp.broadcast_to(index & (LANES - 1), (16, span)).astype(jnp.int16)[0:1]
         hot = jnp.where(
-            points == jnp.broadcast_to(place, (depth, span)), jnp.bfloat16(1), jnp.bfloat16(0)
+            points == jnp.broadcast_to(place, (LANES, span)), jnp.bfloat16(1), jnp.bfloat16(0)
         )
-        values = jnp.dot(left, hot, preferred_element_type=jnp.float32)
-        values = values.reshape(members, levels * half, span) * masked[None]
+        values = jnp.dot(matrix, hot, preferred_element_type=jnp.float32)
+        values = values.reshape(levels * members, blocks, span) * masked[None]
         total = values if k == 0 else total + values
-    summed = None
+    sums = [None] * levels
     for m in range(members):
         p = pert_ref[m, :, cols].astype(jnp.float32)
-        wide = jnp.concatenate(
-            [jnp.broadcast_to(p[l:l + 1], (half, span)) for l in range(levels)], axis=0
-        )
-        summed = total[m] * wide if m == 0 else summed + total[m] * wide
-    return jnp.concatenate(
-        [jnp.sum(summed[l * half:(l + 1) * half], axis=0, keepdims=True) for l in range(levels)], axis=0
-    )
+        for l in range(levels):
+            term = total[l * members + m] * jnp.broadcast_to(p[l:l + 1], wide)
+            sums[l] = term if m == 0 else sums[l] + term
+    return jnp.concatenate([jnp.sum(term, axis=0, keepdims=True) for term in sums], axis=0)
 
 
 def whole_kernel(
@@ -129,14 +119,15 @@
             device_id_type=MESH,
         )
 
-    def columns(owner):
-        return pl.ds(pl.multiple_of(owner * span, LANES), span)
-
-    matrix = jnp.concatenate([table[0], table[1]], axis=1).astype(jnp.bfloat16)
+    matrix = table[...].astype(jnp.bfloat16)
 
     def body(step, carry):
-        cols = columns(lax.rem(me + step, owners))
-        partial[step - 1] = interpolate(matrix, cols, index_ref, weight_ref, pert_ref)
+        first = lax.rem(me + step, owners) * span
+        for at in range(0, span, PIECE):
+            cols = pl.ds(pl.multiple_of(first + at, LANES), PIECE)
+            partial[step - 1, :, at:at + PIECE] = interpolate(
+                matrix, blocks, cols, index_ref, weight_ref, pert_ref
+            )
 
         @pl.when(step < owners)
         def _():
@@ -185,7 +176,7 @@
             pltpu.VMEM(operands[-1].shape, perturbation.dtype),
             pltpu.VMEM((3, lm * blocks, width), jnp.float32),
             pltpu.VMEM((3 * blocks, lm, width), jnp.float32),
-            pltpu.VMEM((2, lm * blocks // 2, width), jnp.float32),
+            pltpu.VMEM((lm * blocks, width), jnp.float32),
             pltpu.VMEM((owners, levels, span), jnp.float32),
             pltpu.VMEM((owners - 1, levels, span), jnp.float32),
             pltpu.SemaphoreType.DMA((len(operands),)),

time: 35.6 us -> 34.6 us (0.972)
  Pallas kernels: 33.4 us -> 32.5 us
    pallas_call x1, Pallas kernels: 33.4 us -> 32.5 us  [per_device(): pl.pallas_call(whole_kernel, out_shape=jax.ShapeDtypeStruct((levels, span...]
where the time goes in v3:
time: 34.6 us; the launch traced here: 34.4 us
  Pallas kernels  32.5 us (94%)
  local copies, waits for them, and re-layouts  1.33 us (4%)
  between operations  0.66 us (2%)
    pallas_call x1, Pallas kernels, per_device(): pl.pallas_call(whole_kernel, out_shape=jax.ShapeDtypeStruct((levels, span...  32.5 us
    unnamed x1, local copies, waits for them, and re-layouts  1.33 us

profile of v3, /device:TPU:1, one launch (start us, length us, event | category | flops | bytes accessed | tf_op | source)
XLA Modules:
  0.0 34.4 jit_solution(17718961612343083455)
XLA Ops:
  0.7 32.5 %shard_map.82 = f32[2,2304]{1,0:T(2,128)} custom-call(bf16[2,10,8,128]{3,2,1,0:T(8,128)(2,1)} %alpha_hbm.1, bf16[12,128,128]{2,1,0:T(8,128)(2,1)} %kernel_hbm.1, s32[12]{0:T(128)} %src_hbm.1, s32[12]{0:T(128)} %dst_hbm.1, s32[1]{0:T(128)S(6)} %copy.10.count_hbm, s32[4,18432]{1,0:T(4,128)} %index_hbm.1, f32[4,18432]{1,0:T(4,128)} %weight_hbm.1, ...), custom_call_target="tpu_custom_call" | custom-call | tf_op jit(solution)/shard_map/pallas_call | solution.py:161
  33.1 1.3 %copy.11 = f32[2,2304]{1,0:T(2,128)} copy(f32[2,2304]{1,0:T(2,128)} %shard_map.82) | data formatting | bytes 36864

commit v4 on v3

--- a/solution.py
+++ b/solution.py
@@ -62,7 +62,7 @@
     alpha_hbm, kernel_hbm, src_hbm, dst_hbm, count_hbm, index_hbm, weight_hbm, pert_hbm, out_ref,
     prev_ref, alpha_ref, next_ref, kernel_ref, src_ref, dst_ref, count_ref, index_ref, weight_ref, pert_ref,
     rows, window, table, partial, slots,
-    load_sem, halo_send, halo_recv, share_send, share_recv,
+    load_sem, ready, halo_send, halo_recv, share_send, share_recv,
 ):
     tiles, owners = lax.axis_size("space"), lax.axis_size("members")
     tile, me = lax.axis_index("space"), lax.axis_index("members")
@@ -71,8 +71,7 @@
     blocks = alpha_ref.shape[2]
 
     barrier = pltpu.get_barrier_semaphore()
-    for neighbour in (left, right):
-        pl.semaphore_signal(barrier, inc=1, device_id={"space": neighbour}, device_id_type=MESH)
+    pl.semaphore_signal(barrier, inc=1, device_id={"space": left}, device_id_type=MESH)
     for step in range(1, owners):
         peer = lax.rem(me + step, owners)
         pl.semaphore_signal(barrier, inc=1, device_id={"members": peer}, device_id_type=MESH)
@@ -86,7 +85,8 @@
         load.start()
         loads.append(load)
 
-    pl.semaphore_wait(barrier, owners + 1)
+    pl.semaphore_wait(barrier, owners)
+    pl.semaphore_signal(ready, inc=1, device_id={"space": right}, device_id_type=MESH)
     halos = []
     for way, (neighbour, landing) in enumerate(((right, prev_ref), (left, next_ref))):
         copy = pltpu.make_async_remote_copy(
@@ -97,6 +97,8 @@
             device_id={"space": neighbour},
             device_id_type=MESH,
         )
+        if way == 1:
+            pl.semaphore_wait(ready, 1)
         copy.start()
         halos.append(copy)
     loads[0].wait()
@@ -180,6 +182,7 @@
             pltpu.VMEM((owners, levels, span), jnp.float32),
             pltpu.VMEM((owners - 1, levels, span), jnp.float32),
             pltpu.SemaphoreType.DMA((len(operands),)),
+            pltpu.SemaphoreType.REGULAR,
             pltpu.SemaphoreType.DMA((2,)),
             pltpu.SemaphoreType.DMA((2,)),
             pltpu.SemaphoreType.DMA((owners - 1,)),

time: 34.6 us -> 34.6 us (level)
  no operation moved by 1% of the time
where the time goes in v4:
time: 34.6 us; the launch traced here: 34.5 us
  Pallas kernels  32.5 us (94%)
  local copies, waits for them, and re-layouts  1.33 us (4%)
  between operations  0.66 us (2%)
    pallas_call x1, Pallas kernels, per_device(): pl.pallas_call(whole_kernel, out_shape=jax.ShapeDtypeStruct((levels, span...  32.5 us
    unnamed x1, local copies, waits for them, and re-layouts  1.33 us

profile of v4, /device:TPU:1, one launch (start us, length us, event | category | flops | bytes accessed | tf_op | source)
XLA Modules:
  0.0 34.5 jit_solution(6159699107408405639)
XLA Ops:
  0.7 32.5 %shard_map.82 = f32[2,2304]{1,0:T(2,128)} custom-call(bf16[2,10,8,128]{3,2,1,0:T(8,128)(2,1)} %alpha_hbm.1, bf16[12,128,128]{2,1,0:T(8,128)(2,1)} %kernel_hbm.1, s32[12]{0:T(128)} %src_hbm.1, s32[12]{0:T(128)} %dst_hbm.1, s32[1]{0:T(128)S(6)} %copy.10.count_hbm, s32[4,18432]{1,0:T(4,128)} %index_hbm.1, f32[4,18432]{1,0:T(4,128)} %weight_hbm.1, ...), custom_call_target="tpu_custom_call" | custom-call | tf_op jit(solution)/shard_map/pallas_call | solution.py:163
  33.1 1.3 %copy.11 = f32[2,2304]{1,0:T(2,128)} copy(f32[2,2304]{1,0:T(2,128)} %shard_map.82) | data formatting | bytes 36864

commit v5 on v4

--- a/solution.py
+++ b/solution.py
@@ -59,15 +59,15 @@
 
 
 def whole_kernel(
-    alpha_hbm, kernel_hbm, src_hbm, dst_hbm, count_hbm, index_hbm, weight_hbm, pert_hbm, out_ref,
+    alpha_hbm, kernel_hbm, src_hbm, dst_hbm, count_hbm, index_hbm, weight_hbm, pert_hbm, shares_ref,
     prev_ref, alpha_ref, next_ref, kernel_ref, src_ref, dst_ref, count_ref, index_ref, weight_ref, pert_ref,
-    rows, window, table, partial, slots,
-    load_sem, ready, halo_send, halo_recv, share_send, share_recv,
+    rows, window, table, partial,
+    load_sem, own_sem, ready, halo_send, halo_recv, share_send, share_recv,
 ):
     tiles, owners = lax.axis_size("space"), lax.axis_size("members")
     tile, me = lax.axis_index("space"), lax.axis_index("members")
     right, left = lax.rem(tile + 1, tiles), lax.rem(tile + tiles - 1, tiles)
-    span = out_ref.shape[1]
+    span = shares_ref.shape[2]
     blocks = alpha_ref.shape[2]
 
     barrier = pltpu.get_barrier_semaphore()
@@ -105,16 +105,16 @@
     stage(alpha_ref, 1, rows, window)
     for load in loads[1:]:
         load.wait()
+    halos[1].wait_recv()
+    stage(next_ref, 2, rows, window)
     halos[0].wait_recv()
     stage(prev_ref, 0, rows, window)
-    halos[1].wait_recv()
-    stage(next_ref, 2, rows, window)
     convolve(src_ref, dst_ref, count_ref, blocks, kernel_ref, window, table)
 
     def share(step):
         return pltpu.make_async_remote_copy(
             src_ref=partial.at[step - 1],
-            dst_ref=slots.at[step - 1],
+            dst_ref=shares_ref.at[step - 1],
             send_sem=share_send.at[step - 1],
             recv_sem=share_recv.at[step - 1],
             device_id={"members": lax.rem(me + step, owners)},
@@ -138,11 +138,11 @@
         return carry
 
     lax.fori_loop(1, owners + 1, body, 0)
-    total = partial[owners - 1]
+    own = pltpu.make_async_copy(partial.at[owners - 1], shares_ref.at[owners - 1], own_sem)
+    own.start()
     for step in range(1, owners):
         share(step).wait_recv()
-        total = total + slots[step - 1]
-    out_ref[...] = total
+    own.wait()
     for step in range(1, owners):
         share(step).wait_send()
     for copy in halos:
@@ -160,11 +160,11 @@
         alpha, kernel, src_index, dst_index, entry_count, interp_index, interp_weight,
         jnp.transpose(perturbation, (1, 0, 2)),
     )
-    return pl.pallas_call(
+    shares = pl.pallas_call(
         whole_kernel,
-        out_shape=jax.ShapeDtypeStruct((levels, span), jnp.float32),
+        out_shape=jax.ShapeDtypeStruct((owners, levels, span), jnp.float32),
         in_specs=[pl.BlockSpec(memory_space=pl.ANY)] * len(operands),
-        out_specs=pl.BlockSpec(memory_space=pltpu.VMEM),
+        out_specs=pl.BlockSpec(memory_space=pl.ANY),
         scratch_shapes=[
             pltpu.VMEM(alpha.shape, alpha.dtype),
             pltpu.VMEM(alpha.shape, alpha.dtype),
@@ -180,8 +180,8 @@
             pltpu.VMEM((3 * blocks, lm, width), jnp.float32),
             pltpu.VMEM((lm * blocks, width), jnp.float32),
             pltpu.VMEM((owners, levels, span), jnp.float32),
-            pltpu.VMEM((owners - 1, levels, span), jnp.float32),
             pltpu.SemaphoreType.DMA((len(operands),)),
+            pltpu.SemaphoreType.DMA,
             pltpu.SemaphoreType.REGULAR,
             pltpu.SemaphoreType.DMA((2,)),
             pltpu.SemaphoreType.DMA((2,)),
@@ -192,6 +192,7 @@
             collective_id=0, has_side_effects=True, vmem_limit_bytes=60 * 1024 * 1024
         ),
     )(*operands)
+    return jnp.sum(shares, axis=0)
 
 
 def solution(mesh):

time: 34.6 us -> 34.3 us (level)
  other arithmetic: 0 us -> 1.57 us
  local copies, waits for them, and re-layouts: 1.33 us -> 0 us
  Pallas kernels: 32.5 us -> 32 us
    reduce_sum x0 -> x1, other arithmetic: none -> 1.57 us  [per_device(): return jnp.sum(shares, axis=0)]
    unnamed x1 -> x0, local copies, waits for them, and re-layouts: 1.33 us -> none
    pallas_call x1, Pallas kernels: 32.5 us -> 32 us  [per_device(): pl.pallas_call(whole_kernel, out_shape=jax.ShapeDtypeStruct((owners, leve...]
where the time goes in v5:
time: 34.3 us; the launch traced here: 34.2 us
  Pallas kernels  32 us (93%)
  other arithmetic  1.57 us (5%)
  between operations  0.66 us (2%)
    pallas_call x1, Pallas kernels, per_device(): pl.pallas_call(whole_kernel, out_shape=jax.ShapeDtypeStruct((owners, leve...  32 us
    reduce_sum x1, other arithmetic, per_device(): return jnp.sum(shares, axis=0)  1.57 us

profile of v5, /device:TPU:1, one launch (start us, length us, event | category | flops | bytes accessed | tf_op | source)
XLA Modules:
  0.0 34.2 jit_solution(4990127849487361753)
XLA Ops:
  0.7 32.0 %shard_map.82 = f32[8,2,2304]{2,1,0:T(2,128)} custom-call(bf16[2,10,8,128]{3,2,1,0:T(8,128)(2,1)} %alpha_hbm.1, bf16[12,128,128]{2,1,0:T(8,128)(2,1)} %kernel_hbm.1, s32[12]{0:T(128)} %src_hbm.1, s32[12]{0:T(128)} %dst_hbm.1, s32[1]{0:T(128)S(6)} %copy.9.count_hbm, s32[4,18432]{1,0:T(4,128)} %index_hbm.1, f32[4,18432]{1,0:T(4,128)} %weight_hbm.1, ...), custom_call_target="tpu_custom_call" | custom-call | tf_op jit(solution)/shard_map/pallas_call | solution.py:163
  32.6 1.6 %reduce_sum.9 = f32[2,2304]{1,0:T(2,128)} reduce(f32[8,2,2304]{2,1,0:T(2,128)} %shard_map.82, f32[]{:T(128)} %constant.0.clone.1), dimensions={0}, to_apply=%region_0.0 | reduce | flops 32256 | bytes 165892 | tf_op jit(solution)/shard_map/reduce_sum | solution.py:195
